TPU v7x, 256 devices: a whole 4x4x8 slice. The times are simulated.
256 devices in a mesh: dp: 4 (over z_lo), seq: 16 (over z_hi, x, core), head: 4 (over y).
Axes of the slice: x: 4, y: 4, z: 8 (z_hi: 2, z_lo: 4; z = z_hi * 4 + z_lo), core: 2. Of those that a mesh axis runs over, the one named last changes fastest.
Arguments:
- queries: bfloat16 [4, 2048, 4096], P('dp', 'seq', 'head'), may hold values from -8 to 8
- keys: bfloat16 [4, 2048, 1024], P('dp', 'seq', 'head'), may hold values from -8 to 8
- values: bfloat16 [4, 2048, 1024], P('dp', 'seq', 'head'), may hold values from -6 to 6
- grad_out: bfloat16 [4, 2048, 4096], P('dp', 'seq', 'head'), may hold values from -6 to 6
- doc_ids: int32 [4, 2048], P('dp', 'seq'), may hold values from 0 to 7, never falling along the last dimension, each value on 1 to 1536 neighbouring positions
- out_weight: bfloat16 [4096, 4096], P('head'), may hold values from -0.09375 to 0.09375
Outputs:
- layer_out: float32 [4, 2048, 4096], P('dp', 'seq', 'head')
- grad_queries: float32 [4, 2048, 4096], P('dp', 'seq', 'head')
- grad_keys: float32 [4, 2048, 1024], P('dp', 'seq', 'head')
- grad_values: float32 [4, 2048, 1024], P('dp', 'seq', 'head')
- weight_grad: float32 [4096, 4096], P('head', 'seq')
Inputs may be any that keep to these rules, and one draw needn't show every extreme that they name: `doc_ids`: never falling along a sequence; every number names a document of 1 to 1536 positions, and one document of each sequence has exactly 1536.
All inputs are finite; a program needn't handle non-finite values.
Results may differ from a plain program's by a relative error of at most 0.035.
Values may be sent and summed in bfloat16 or wider, within the bound.
No kernel may reach another device: no remote copies, remote signals or barrier semaphores. Data moves between devices by JAX's collectives and lax.ppermute only.
A program may use at most 128 MiB of HBM per device.

v0:
```python
from functools import partial

import jax
import jax.numpy as jnp
from jax import lax
from jax.sharding import PartitionSpec as P

HEAD_SIZE = 128


def shifted(value, axis, by):
    devices = lax.axis_size(axis)
    return lax.ppermute(value, axis, [(i, (i + by) % devices) for i in range(devices)])


def visible(query_doc, query_pos, key_doc, key_pos):
    return (query_doc[:, None] == key_doc[None, :]) & (key_pos[None, :] <= query_pos[:, None])


def forward_tile(query_matrix, query_doc, query_pos, scale, carry, piece):
    key_matrix, value_matrix, key_doc, key_pos = piece
    allowed = visible(query_doc, query_pos, key_doc, key_pos)

    def forward_compute(state):
        run_max, run_sum, run_acc = state
        scores = (
            jnp.einsum(
                "rkgd,pkd->kgrp", query_matrix, key_matrix, preferred_element_type=jnp.float32
            )
            * scale
        )
        scores = jnp.where(allowed[None, None], scores, -jnp.inf)
        new_max = jnp.max(scores, axis=-1)
        safe_max = jnp.where(new_max == -jnp.inf, 0.0, new_max)
        factor = jnp.exp(run_max - safe_max)
        weights = jnp.exp(scores - safe_max[..., None])
        new_sum = run_sum * factor + jnp.sum(weights, axis=-1)
        update = jnp.einsum(
            "kgrp,pkd->rkgd",
            weights,
            value_matrix.astype(jnp.float32),
            precision=lax.Precision.HIGHEST,
            preferred_element_type=jnp.float32,
        )
        return (new_max, new_sum, run_acc * factor.transpose(2, 0, 1)[..., None] + update)

    return lax.cond(jnp.any(allowed), forward_compute, lambda state: state, carry)


def backward_tile(
    query_matrix, head_gradient, log_total, delta, query_doc, query_pos, scale, block
):
    key_matrix, value_matrix, key_doc, key_pos = block
    allowed = visible(query_doc, query_pos, key_doc, key_pos)

    def backward_compute(unused):
        scores = (
            jnp.einsum(
                "rkgd,pkd->kgrp", query_matrix, key_matrix, preferred_element_type=jnp.float32
            )
            * scale
        )
        probs = jnp.where(allowed[None, None], jnp.exp(scores - log_total[..., None]), 0.0)
        grad_v = jnp.einsum(
            "kgrp,rkgd->pkd",
            probs.astype(jnp.bfloat16),
            head_gradient,
            preferred_element_type=jnp.float32,
        )
        grad_p = jnp.einsum(
            "rkgd,pkd->kgrp", head_gradient, value_matrix, preferred_element_type=jnp.float32
        )
        grad_s = (scale * probs * (grad_p - delta[..., None])).astype(jnp.bfloat16)
        grad_q = jnp.einsum(
            "kgrp,pkd->rkgd", grad_s, key_matrix, preferred_element_type=jnp.float32
        )
        grad_k = jnp.einsum(
            "kgrp,rkgd->pkd", grad_s, query_matrix, preferred_element_type=jnp.float32
        )
        return (grad_q, grad_k, grad_v)

    def skip(unused):
        return (
            jnp.zeros(query_matrix.shape, jnp.float32),
            jnp.zeros(key_matrix.shape, jnp.float32),
            jnp.zeros(value_matrix.shape, jnp.float32),
        )

    return lax.cond(jnp.any(allowed), backward_compute, skip, 0)


def shards(queries, keys, values, grad_out, doc_ids, out_weight):
    rows = queries.shape[1]
    depth = out_weight.shape[0]
    kv_local = keys.shape[2] // HEAD_SIZE
    query_group = depth // HEAD_SIZE // kv_local
    scale = HEAD_SIZE ** (-0.5)
    count = lax.axis_size("seq")
    index = lax.axis_index("seq")
    offsets = jnp.arange(rows, dtype=jnp.int32)
    positions = index * rows + offsets
    query_matrix = queries[0].reshape(rows, kv_local, query_group, HEAD_SIZE)
    key_matrix = keys[0].reshape(rows, kv_local, HEAD_SIZE)
    value_matrix = values[0].reshape(rows, kv_local, HEAD_SIZE)
    query_doc = doc_ids[0]
    start_state = (
        jnp.full((kv_local, query_group, rows), -jnp.inf, jnp.float32),
        jnp.zeros((kv_local, query_group, rows), jnp.float32),
        jnp.zeros((rows, kv_local, query_group, HEAD_SIZE), jnp.float32),
    )
    run_max, run_sum, run_acc = forward_tile(
        query_matrix,
        query_doc,
        positions,
        scale,
        start_state,
        (
            lax.all_gather(key_matrix, "seq", axis=0, tiled=True),
            lax.all_gather(value_matrix, "seq", axis=0, tiled=True),
            lax.all_gather(query_doc, "seq", axis=0, tiled=True),
            lax.all_gather(positions, "seq", axis=0, tiled=True),
        ),
    )
    heads_out = (run_acc / run_sum.transpose(2, 0, 1)[..., None]).astype(jnp.bfloat16)
    log_total = run_max + jnp.log(run_sum)
    heads_flat = heads_out.reshape(rows, depth)
    out_terms = jnp.dot(heads_flat, out_weight, preferred_element_type=jnp.float32)
    layer_out = lax.psum_scatter(out_terms, "head", scatter_dimension=1, tiled=True)
    full_grad = lax.all_gather(grad_out[0], "head", axis=1, tiled=True)
    head_gradient = lax.dot_general(
        full_grad, out_weight, (((1,), (1,)), ((), ())), preferred_element_type=jnp.float32
    ).astype(jnp.bfloat16)
    head_gradient = head_gradient.reshape(rows, kv_local, query_group, HEAD_SIZE)
    delta = jnp.sum(
        head_gradient.astype(jnp.float32) * heads_out.astype(jnp.float32), axis=-1
    ).transpose(1, 2, 0)
    weight_part = lax.psum_scatter(
        lax.dot_general(
            full_grad, heads_flat, (((0,), (0,)), ((), ())), preferred_element_type=jnp.float32
        ),
        "seq",
        scatter_dimension=0,
        tiled=True,
    )
    weight_grad = lax.psum(weight_part, "dp").T
    tile = partial(
        backward_tile, query_matrix, head_gradient, log_total, delta, query_doc, positions, scale
    )
    zeros_q = jnp.zeros(query_matrix.shape, jnp.float32)

    def cycle_step(step, state):
        key_now, value_now, doc_now, pos_now, grad_k, grad_v, grad_q = state
        add_q, add_k, add_v = tile((key_now, value_now, doc_now, pos_now))
        moved = (
            shifted(key_now.astype(jnp.float32), "seq", 1).astype(key_now.dtype),
            shifted(value_now.astype(jnp.float32), "seq", 1).astype(value_now.dtype),
            shifted(doc_now, "seq", 1),
            shifted(pos_now, "seq", 1),
            shifted(grad_k + add_k, "seq", 1),
            shifted(grad_v + add_v, "seq", 1),
        )
        return tuple(moved) + (grad_q + add_q,)

    final = lax.fori_loop(
        0,
        count,
        cycle_step,
        (
            key_matrix,
            value_matrix,
            query_doc,
            positions,
            jnp.zeros(key_matrix.shape, jnp.float32),
            jnp.zeros(value_matrix.shape, jnp.float32),
            zeros_q,
        ),
    )
    grad_k, grad_v, grad_q = (final[4], final[5], final[6])
    grad_query = grad_q.reshape(rows, depth)
    key_gradient = grad_k.reshape(rows, kv_local * HEAD_SIZE)
    value_gradient = grad_v.reshape(rows, kv_local * HEAD_SIZE)
    return (
        layer_out[None],
        grad_query[None],
        key_gradient[None],
        value_gradient[None],
        weight_grad,
    )


def solution(mesh):
    placed = (
        P("dp", "seq", "head"),
        P("dp", "seq", "head"),
        P("dp", "seq", "head"),
        P("dp", "seq", "head"),
        P("dp", "seq"),
        P("head", None),
    )
    return jax.shard_map(
        shards,
        mesh=mesh,
        in_specs=placed,
        out_specs=(
            P("dp", "seq", "head"),
            P("dp", "seq", "head"),
            P("dp", "seq", "head"),
            P("dp", "seq", "head"),
            P("head", "seq"),
        ),
        check_vma=False,
    )
```

profile of v0, /device:TPU:56, one launch (start us, length us, event | category | flops | bytes accessed | tf_op | source)
XLA Modules:
  0.0 781.4 jit_solution(12665137972576970)
XLA Ops:
  12.4 32.1 %all-gather.2 = s32[16,1,128]{2,1,0:T(1,128)S(1)} all-gather(s32[1,1,128]{2,1,0:T(1,128)S(1)} %fusion.32), channel_id=1, replica_groups=mesh['dp'=4,'seq'=16,'head'=4] {'seq'}, dimensions={0}, use_global_device_ids=true | all-gather | bytes 8704 | tf_op jit(solution)/shard_map/all_gather | solution.py:121
  44.5 24.1 %all-gather = s32[1,2048]{1,0:T(1,128)S(1)} all-gather(s32[1,128]{1,0:T(1,128)} %param.16), channel_id=2, replica_groups=mesh['dp'=4,'seq'=16,'head'=4] {'seq'}, dimensions={1}, use_global_device_ids=true | all-gather | bytes 8704 | tf_op jit(solution)/shard_map/all_gather | solution.py:120
  78.9 18.4 %all-gather.7.cloned.1.call-done = bf16[2048,2,128]{0,2,1:T(8,128)(2,1)} async-done(((bf16[128,2,128]{0,2,1:T(8,128)(2,1)}), bf16[2048,2,128]{0,2,1:T(8,128)(2,1)}) %all-gather.7.cloned.1.call-update) | async-done | bytes 1048592 | tf_op jit(solution)/shard_map/all_gather | solution.py:118
  97.3 54.8 %all-gather.9.cloned.1.call-done = bf16[2048,2,128]{0,2,1:T(8,128)(2,1)} async-done(((bf16[128,2,128]{0,2,1:T(8,128)(2,1)}), bf16[2048,2,128]{0,2,1:T(8,128)(2,1)}) %all-gather.9.cloned.1.call-update) | async-done | bytes 1048592 | tf_op jit(solution)/shard_map/all_gather | solution.py:119
  152.1 20.3 %conditional.2 = (f32[2,4,128]{2,1,0:T(4,128)}, f32[2,4,128]{2,1,0:T(4,128)S(1)}, f32[2,4,128]{2,1,0:T(4,128)S(1)}, f32[128,2,4,128]{0,3,2,1:T(8,128)S(1)}) conditional(s32[]{:T(128)} %convert_element_type.37, () %tuple.30, (pred[128,2048]{0,1:T(8,128)(4,1)S(1)}, bf16[2048,2,128]{0,2,1:T(8,128)(2,1)}, bf16[128,2,4,128]{0,3,2,1:T(8,128)(2,1)S(1)}, ...), branch_computations={%region_1.0_spmd, %region_2.5_spmd} | conditional | flops 3779208192 | bytes 67686488 | solution.py:47
  188.0 210.2 %reduce-scatter.5.cloned.1.call-done = f32[256,1024]{0,1:T(8,128)} async-done(((f32[4096,1024]{0,1:T(8,128)}), f32[256,1024]{0,1:T(8,128)}) %reduce-scatter.5.cloned.1.call-update) | async-done | bytes 1048592 | tf_op jit(solution)/shard_map/reduce_scatter | solution.py:137
  398.3 371.0 %while.23 = (s32[]{:T(128)}, bf16[128,2,128]{2,0,1:T(8,128)(2,1)S(1)}, bf16[128,2,128]{2,0,1:T(8,128)(2,1)S(1)}, s32[128]{0:T(128)S(1)}, s32[128]{0:T(128)S(1)},...) while((s32[]{:T(128)}, ...), condition=%wide.region_11.12_spmd.clone, body=%wide.region_7.11_spmd.clone.sunk | while | flops 169214080 | bytes 8635369 | solution.py:164
  424.2 8.4 %collective-permute-done.2 = s32[128]{0:T(128)S(1)} collective-permute-done((s32[128]{0:T(128)S(1)}, s32[128]{0:T(128)S(1)}, u32[]{:S(2)}, u32[]{:S(2)}) %collective-permute-start.2) | collective-permute-done | bytes 544 | tf_op jit(solution)/shard_map/while/body/eval_jaxpr/ppermute | solution.py:13
  446.0 16.4 %collective-permute-done.2 = s32[128]{0:T(128)S(1)} collective-permute-done((s32[128]{0:T(128)S(1)}, s32[128]{0:T(128)S(1)}, u32[]{:S(2)}, u32[]{:S(2)}) %collective-permute-start.2) | collective-permute-done | bytes 544 | tf_op jit(solution)/shard_map/while/body/eval_jaxpr/ppermute | solution.py:13
  478.4 8.4 %collective-permute-done.2 = s32[128]{0:T(128)S(1)} collective-permute-done((s32[128]{0:T(128)S(1)}, s32[128]{0:T(128)S(1)}, u32[]{:S(2)}, u32[]{:S(2)}) %collective-permute-start.2) | collective-permute-done | bytes 544 | tf_op jit(solution)/shard_map/while/body/eval_jaxpr/ppermute | solution.py:13
  487.0 12.2 %collective-permute-done.4 = f32[128,2,128]{2,0,1:T(8,128)S(1)} collective-permute-done((f32[128,2,128]{2,0,1:T(8,128)S(1)}, f32[128,2,128]{2,0,1:T(8,128)S(1)}, u32[]{:S(2)}, u32[]{:S(2)}) %collective-permute-start.4) | collective-permute-done | bytes 131104 | tf_op jit(solution)/shard_map/while/body/eval_jaxpr/ppermute | solution.py:13
  510.2 9.5 %collective-permute-done.2 = s32[128]{0:T(128)S(1)} collective-permute-done((s32[128]{0:T(128)S(1)}, s32[128]{0:T(128)S(1)}, u32[]{:S(2)}, u32[]{:S(2)}) %collective-permute-start.2) | collective-permute-done | bytes 544 | tf_op jit(solution)/shard_map/while/body/eval_jaxpr/ppermute | solution.py:13
  533.2 8.4 %collective-permute-done.2 = s32[128]{0:T(128)S(1)} collective-permute-done((s32[128]{0:T(128)S(1)}, s32[128]{0:T(128)S(1)}, u32[]{:S(2)}, u32[]{:S(2)}) %collective-permute-start.2) | collective-permute-done | bytes 544 | tf_op jit(solution)/shard_map/while/body/eval_jaxpr/ppermute | solution.py:13
  555.0 8.3 %collective-permute-done.2 = s32[128]{0:T(128)S(1)} collective-permute-done((s32[128]{0:T(128)S(1)}, s32[128]{0:T(128)S(1)}, u32[]{:S(2)}, u32[]{:S(2)}) %collective-permute-start.2) | collective-permute-done | bytes 544 | tf_op jit(solution)/shard_map/while/body/eval_jaxpr/ppermute | solution.py:13
  576.7 8.3 %collective-permute-done.2 = s32[128]{0:T(128)S(1)} collective-permute-done((s32[128]{0:T(128)S(1)}, s32[128]{0:T(128)S(1)}, u32[]{:S(2)}, u32[]{:S(2)}) %collective-permute-start.2) | collective-permute-done | bytes 544 | tf_op jit(solution)/shard_map/while/body/eval_jaxpr/ppermute | solution.py:13
  598.5 8.3 %collective-permute-done.2 = s32[128]{0:T(128)S(1)} collective-permute-done((s32[128]{0:T(128)S(1)}, s32[128]{0:T(128)S(1)}, u32[]{:S(2)}, u32[]{:S(2)}) %collective-permute-start.2) | collective-permute-done | bytes 544 | tf_op jit(solution)/shard_map/while/body/eval_jaxpr/ppermute | solution.py:13
  620.2 8.3 %collective-permute-done.2 = s32[128]{0:T(128)S(1)} collective-permute-done((s32[128]{0:T(128)S(1)}, s32[128]{0:T(128)S(1)}, u32[]{:S(2)}, u32[]{:S(2)}) %collective-permute-start.2) | collective-permute-done | bytes 544 | tf_op jit(solution)/shard_map/while/body/eval_jaxpr/ppermute | solution.py:13
  641.9 8.3 %collective-permute-done.2 = s32[128]{0:T(128)S(1)} collective-permute-done((s32[128]{0:T(128)S(1)}, s32[128]{0:T(128)S(1)}, u32[]{:S(2)}, u32[]{:S(2)}) %collective-permute-start.2) | collective-permute-done | bytes 544 | tf_op jit(solution)/shard_map/while/body/eval_jaxpr/ppermute | solution.py:13
  663.6 8.3 %collective-permute-done.2 = s32[128]{0:T(128)S(1)} collective-permute-done((s32[128]{0:T(128)S(1)}, s32[128]{0:T(128)S(1)}, u32[]{:S(2)}, u32[]{:S(2)}) %collective-permute-start.2) | collective-permute-done | bytes 544 | tf_op jit(solution)/shard_map/while/body/eval_jaxpr/ppermute | solution.py:13
  685.4 8.3 %collective-permute-done.2 = s32[128]{0:T(128)S(1)} collective-permute-done((s32[128]{0:T(128)S(1)}, s32[128]{0:T(128)S(1)}, u32[]{:S(2)}, u32[]{:S(2)}) %collective-permute-start.2) | collective-permute-done | bytes 544 | tf_op jit(solution)/shard_map/while/body/eval_jaxpr/ppermute | solution.py:13
  707.1 8.3 %collective-permute-done.2 = s32[128]{0:T(128)S(1)} collective-permute-done((s32[128]{0:T(128)S(1)}, s32[128]{0:T(128)S(1)}, u32[]{:S(2)}, u32[]{:S(2)}) %collective-permute-start.2) | collective-permute-done | bytes 544 | tf_op jit(solution)/shard_map/while/body/eval_jaxpr/ppermute | solution.py:13
  728.8 8.3 %collective-permute-done.2 = s32[128]{0:T(128)S(1)} collective-permute-done((s32[128]{0:T(128)S(1)}, s32[128]{0:T(128)S(1)}, u32[]{:S(2)}, u32[]{:S(2)}) %collective-permute-start.2) | collective-permute-done | bytes 544 | tf_op jit(solution)/shard_map/while/body/eval_jaxpr/ppermute | solution.py:13
  750.5 8.3 %collective-permute-done.2 = s32[128]{0:T(128)S(1)} collective-permute-done((s32[128]{0:T(128)S(1)}, s32[128]{0:T(128)S(1)}, u32[]{:S(2)}, u32[]{:S(2)}) %collective-permute-start.2) | collective-permute-done | bytes 544 | tf_op jit(solution)/shard_map/while/body/eval_jaxpr/ppermute | solution.py:13
  760.9 8.3 %collective-permute-done.5 = f32[128,2,128]{2,0,1:T(8,128)S(1)} collective-permute-done((f32[128,2,128]{2,0,1:T(8,128)S(1)}, f32[128,2,128]{2,0,1:T(8,128)S(1)}, u32[]{:S(2)}, u32[]{:S(2)}) %collective-permute-start.5) | collective-permute-done | bytes 131104 | tf_op jit(solution)/shard_map/while/body/eval_jaxpr/ppermute | solution.py:13
  (447 shorter events, 264.7 us)
Async XLA Ops:
  7.2 64.7 %all-gather.11.cloned.1.call-start = ((), (), s32[]{:S(2)}) async-start(), calls=%async_computation.7 | async-start | bytes 1310720 | tf_op jit(solution)/shard_map/all_gather | solution.py:129
  7.9 89.4 %all-gather.7.cloned.1.call-start = ((), (), s32[]{:S(2)}) async-start(), calls=%async_computation.2 | async-start | bytes 1114112 | tf_op jit(solution)/shard_map/all_gather | solution.py:118
  9.5 142.5 %all-gather.9.cloned.1.call-start = ((), (), s32[]{:S(2)}) async-start(), calls=%async_computation.3 | async-start | bytes 1114112 | tf_op jit(solution)/shard_map/all_gather | solution.py:119
  11.2 387.0 %reduce-scatter.5.cloned.1.call-start = ((), (), s32[]{:S(2)}) async-start(), calls=%async_computation.5 | async-start | bytes 17825792 | tf_op jit(solution)/shard_map/reduce_scatter | solution.py:137
  180.6 591.7 %reduce-scatter.3.cloned.1.call-start = ((), (), s32[]{:S(2)}) async-start(), calls=%async_computation.4 | async-start | bytes 2621440 | tf_op jit(solution)/shard_map/reduce_scatter | solution.py:128
  186.7 585.6 %all-reduce.2.cloned.1.call-start = ((), (), s32[]{:S(2)}) async-start(), calls=%async_computation.6 | async-start | bytes 2097152 | tf_op jit(solution)/shard_map/psum | solution.py:145
  424.1 14.4 %collective-permute-start.4 = (f32[128,2,128]{2,0,1:T(8,128)S(1)}, f32[128,2,128]{2,0,1:T(8,128)S(1)}, u32[]{:S(2)}, u32[]{:S(2)}) collective-permute-start(f32[128,2,128]{2,0,1:T(8,128)S(1)} %add.74), channel_id=1, source_target_pairs={{0,4},{4,8},{8,12},{12,16},{16,20},{20,24},{24,28},{28,32},{32,36}... | collective-permute-start | bytes 393224 | tf_op jit(solution)/shard_map/while/body/eval_jaxpr/ppermute | solution.py:13
  443.7 19.0 %collective-permute-start = (bf16[128,2,128]{2,0,1:T(8,128)(2,1)}, bf16[128,2,128]{2,0,1:T(8,128)(2,1)S(1)}, u32[]{:S(2)}, u32[]{:S(2)}) collective-permute-start(bf16[128,2,128]{2,0,1:T(8,128)(2,1)} %copy.90), channel_id=1, source_target_pairs={{0,4},{4,8},{8,12},{12,16},{16,20},{20,24},{24,28},{28,32},{32,36}... | collective-permute-start | bytes 196616 | tf_op jit(solution)/shard_map/while/body/eval_jaxpr/ppermute | solution.py:13
  444.3 18.4 %collective-permute-start.1 = (bf16[128,2,128]{2,0,1:T(8,128)(2,1)}, bf16[128,2,128]{2,0,1:T(8,128)(2,1)S(1)}, u32[]{:S(2)}, u32[]{:S(2)}) collective-permute-start(bf16[128,2,128]{2,0,1:T(8,128)(2,1)} %copy.91), channel_id=1, source_target_pairs={{0,4},{4,8},{8,12},{12,16},{16,20},{20,24},{24,28},{28,32},{32,36}... | collective-permute-start | bytes 196616 | tf_op jit(solution)/shard_map/while/body/eval_jaxpr/ppermute | solution.py:13
  444.3 18.2 %collective-permute-start.2 = (s32[128]{0:T(128)S(1)}, s32[128]{0:T(128)S(1)}, u32[]{:S(2)}, u32[]{:S(2)}) collective-permute-start(s32[128]{0:T(128)S(1)} %copy.92), channel_id=1, source_target_pairs={{0,4},{4,8},{8,12},{12,16},{16,20},{20,24},{24,28},{28,32},{32,36}... | collective-permute-start | bytes 1544 | tf_op jit(solution)/shard_map/while/body/eval_jaxpr/ppermute | solution.py:13
  444.3 18.3 %collective-permute-start.3 = (s32[128]{0:T(128)S(1)}, s32[128]{0:T(128)S(1)}, u32[]{:S(2)}, u32[]{:S(2)}) collective-permute-start(s32[128]{0:T(128)S(1)} %copy.93), channel_id=1, source_target_pairs={{0,4},{4,8},{8,12},{12,16},{16,20},{20,24},{24,28},{28,32},{32,36}... | collective-permute-start | bytes 1544 | tf_op jit(solution)/shard_map/while/body/eval_jaxpr/ppermute | solution.py:13
  445.9 24.9 %collective-permute-start.4 = (f32[128,2,128]{2,0,1:T(8,128)S(1)}, f32[128,2,128]{2,0,1:T(8,128)S(1)}, u32[]{:S(2)}, u32[]{:S(2)}) collective-permute-start(f32[128,2,128]{2,0,1:T(8,128)S(1)} %add.74), channel_id=1, source_target_pairs={{0,4},{4,8},{8,12},{12,16},{16,20},{20,24},{24,28},{28,32},{32,36}... | collective-permute-start | bytes 393224 | tf_op jit(solution)/shard_map/while/body/eval_jaxpr/ppermute | solution.py:13
  462.4 12.9 %collective-permute-start.5 = (f32[128,2,128]{2,0,1:T(8,128)S(1)}, f32[128,2,128]{2,0,1:T(8,128)S(1)}, u32[]{:S(2)}, u32[]{:S(2)}) collective-permute-start(f32[128,2,128]{2,0,1:T(8,128)S(1)} %add.75), channel_id=1, source_target_pairs={{0,4},{4,8},{8,12},{12,16},{16,20},{20,24},{24,28},{28,32},{32,36}... | collective-permute-start | bytes 393224 | tf_op jit(solution)/shard_map/while/body/eval_jaxpr/ppermute | solution.py:13
  478.3 20.9 %collective-permute-start.4 = (f32[128,2,128]{2,0,1:T(8,128)S(1)}, f32[128,2,128]{2,0,1:T(8,128)S(1)}, u32[]{:S(2)}, u32[]{:S(2)}) collective-permute-start(f32[128,2,128]{2,0,1:T(8,128)S(1)} %add.74), channel_id=1, source_target_pairs={{0,4},{4,8},{8,12},{12,16},{16,20},{20,24},{24,28},{28,32},{32,36}... | collective-permute-start | bytes 393224 | tf_op jit(solution)/shard_map/while/body/eval_jaxpr/ppermute | solution.py:13
  486.8 20.4 %collective-permute-start.5 = (f32[128,2,128]{2,0,1:T(8,128)S(1)}, f32[128,2,128]{2,0,1:T(8,128)S(1)}, u32[]{:S(2)}, u32[]{:S(2)}) collective-permute-start(f32[128,2,128]{2,0,1:T(8,128)S(1)} %add.75), channel_id=1, source_target_pairs={{0,4},{4,8},{8,12},{12,16},{16,20},{20,24},{24,28},{28,32},{32,36}... | collective-permute-start | bytes 393224 | tf_op jit(solution)/shard_map/while/body/eval_jaxpr/ppermute | solution.py:13
  510.1 14.2 %collective-permute-start.4 = (f32[128,2,128]{2,0,1:T(8,128)S(1)}, f32[128,2,128]{2,0,1:T(8,128)S(1)}, u32[]{:S(2)}, u32[]{:S(2)}) collective-permute-start(f32[128,2,128]{2,0,1:T(8,128)S(1)} %add.74), channel_id=1, source_target_pairs={{0,4},{4,8},{8,12},{12,16},{16,20},{20,24},{24,28},{28,32},{32,36}... | collective-permute-start | bytes 393224 | tf_op jit(solution)/shard_map/while/body/eval_jaxpr/ppermute | solution.py:13
  533.1 14.2 %collective-permute-start.4 = (f32[128,2,128]{2,0,1:T(8,128)S(1)}, f32[128,2,128]{2,0,1:T(8,128)S(1)}, u32[]{:S(2)}, u32[]{:S(2)}) collective-permute-start(f32[128,2,128]{2,0,1:T(8,128)S(1)} %add.74), channel_id=1, source_target_pairs={{0,4},{4,8},{8,12},{12,16},{16,20},{20,24},{24,28},{28,32},{32,36}... | collective-permute-start | bytes 393224 | tf_op jit(solution)/shard_map/while/body/eval_jaxpr/ppermute | solution.py:13
  554.9 14.2 %collective-permute-start.4 = (f32[128,2,128]{2,0,1:T(8,128)S(1)}, f32[128,2,128]{2,0,1:T(8,128)S(1)}, u32[]{:S(2)}, u32[]{:S(2)}) collective-permute-start(f32[128,2,128]{2,0,1:T(8,128)S(1)} %add.74), channel_id=1, source_target_pairs={{0,4},{4,8},{8,12},{12,16},{16,20},{20,24},{24,28},{28,32},{32,36}... | collective-permute-start | bytes 393224 | tf_op jit(solution)/shard_map/while/body/eval_jaxpr/ppermute | solution.py:13
  576.6 15.4 %collective-permute-start.4 = (f32[128,2,128]{2,0,1:T(8,128)S(1)}, f32[128,2,128]{2,0,1:T(8,128)S(1)}, u32[]{:S(2)}, u32[]{:S(2)}) collective-permute-start(f32[128,2,128]{2,0,1:T(8,128)S(1)} %add.74), channel_id=1, source_target_pairs={{0,4},{4,8},{8,12},{12,16},{16,20},{20,24},{24,28},{28,32},{32,36}... | collective-permute-start | bytes 393224 | tf_op jit(solution)/shard_map/while/body/eval_jaxpr/ppermute | solution.py:13
  598.4 15.6 %collective-permute-start.4 = (f32[128,2,128]{2,0,1:T(8,128)S(1)}, f32[128,2,128]{2,0,1:T(8,128)S(1)}, u32[]{:S(2)}, u32[]{:S(2)}) collective-permute-start(f32[128,2,128]{2,0,1:T(8,128)S(1)} %add.74), channel_id=1, source_target_pairs={{0,4},{4,8},{8,12},{12,16},{16,20},{20,24},{24,28},{28,32},{32,36}... | collective-permute-start | bytes 393224 | tf_op jit(solution)/shard_map/while/body/eval_jaxpr/ppermute | solution.py:13
  620.1 15.6 %collective-permute-start.4 = (f32[128,2,128]{2,0,1:T(8,128)S(1)}, f32[128,2,128]{2,0,1:T(8,128)S(1)}, u32[]{:S(2)}, u32[]{:S(2)}) collective-permute-start(f32[128,2,128]{2,0,1:T(8,128)S(1)} %add.74), channel_id=1, source_target_pairs={{0,4},{4,8},{8,12},{12,16},{16,20},{20,24},{24,28},{28,32},{32,36}... | collective-permute-start | bytes 393224 | tf_op jit(solution)/shard_map/while/body/eval_jaxpr/ppermute | solution.py:13
  641.8 15.6 %collective-permute-start.4 = (f32[128,2,128]{2,0,1:T(8,128)S(1)}, f32[128,2,128]{2,0,1:T(8,128)S(1)}, u32[]{:S(2)}, u32[]{:S(2)}) collective-permute-start(f32[128,2,128]{2,0,1:T(8,128)S(1)} %add.74), channel_id=1, source_target_pairs={{0,4},{4,8},{8,12},{12,16},{16,20},{20,24},{24,28},{28,32},{32,36}... | collective-permute-start | bytes 393224 | tf_op jit(solution)/shard_map/while/body/eval_jaxpr/ppermute | solution.py:13
  663.5 15.6 %collective-permute-start.4 = (f32[128,2,128]{2,0,1:T(8,128)S(1)}, f32[128,2,128]{2,0,1:T(8,128)S(1)}, u32[]{:S(2)}, u32[]{:S(2)}) collective-permute-start(f32[128,2,128]{2,0,1:T(8,128)S(1)} %add.74), channel_id=1, source_target_pairs={{0,4},{4,8},{8,12},{12,16},{16,20},{20,24},{24,28},{28,32},{32,36}... | collective-permute-start | bytes 393224 | tf_op jit(solution)/shard_map/while/body/eval_jaxpr/ppermute | solution.py:13
  685.2 15.6 %collective-permute-start.4 = (f32[128,2,128]{2,0,1:T(8,128)S(1)}, f32[128,2,128]{2,0,1:T(8,128)S(1)}, u32[]{:S(2)}, u32[]{:S(2)}) collective-permute-start(f32[128,2,128]{2,0,1:T(8,128)S(1)} %add.74), channel_id=1, source_target_pairs={{0,4},{4,8},{8,12},{12,16},{16,20},{20,24},{24,28},{28,32},{32,36}... | collective-permute-start | bytes 393224 | tf_op jit(solution)/shard_map/while/body/eval_jaxpr/ppermute | solution.py:13
  (84 other events, 865.7 us)
Sparse Core Ops, SparseCore 0:
  9.8 27.5 all-gather.10
  40.5 56.7 all-gather.6
  100.4 51.6 all-gather.8
  180.7 217.4 reduce-scatter.4
  401.3 25.9 reduce-scatter.2
  429.9 71.7 all-reduce.1
where the time goes:
time: 784 us; the launch traced here: 781 us
  waiting for transfers between devices  598 us (76%)
  blocking collectives  56.3 us (7%)
  matrix products  35.2 us (4%)
  local copies, waits for them, and re-layouts  33.6 us (4%)
  other arithmetic  25.6 us (3%)
  between operations  14.9 us (2%)
  loops' own time  12.7 us (2%)
    ppermute x96, waiting for transfers between devices, shifted(): lax.ppermute(value, axis, [(i, (i + by) % devices) for i in range(devices)])  314 us
    reduce_scatter x1, waiting for transfers between devices, shards(): lax.psum_scatter(lax.dot_general(full_grad, heads_flat, (((0,), (0,)), ((...  210 us
    all_gather x1, waiting for transfers between devices, shards(): lax.all_gather(value_matrix, 'seq', axis=0, tiled=True)  54.8 us
    all_gather x1, blocking collectives, shards(): lax.all_gather(positions, 'seq', axis=0, tiled=True)  32.1 us
    all_gather x1, blocking collectives, shards(): lax.all_gather(query_doc, 'seq', axis=0, tiled=True)  24.1 us
    while x64, local copies, waits for them, and re-layouts  20.2 us
    all_gather x1, waiting for transfers between devices, shards(): lax.all_gather(key_matrix, 'seq', axis=0, tiled=True)  18.4 us
  transfers between devices with their start and end apart: 102, of which 51 were waited for; matrix products, arithmetic and copies ran while one was open for 8% of the time, Pallas kernels for 0%

commit v1 on v0

v1 whole, which is shorter than its diff:
```python
import functools

import jax
import jax.numpy as jnp
from jax import lax
from jax.experimental import pallas as pl
from jax.experimental.pallas import tpu as pltpu
from jax.sharding import PartitionSpec as P

HEAD = 128
ROWS = 128
NEG = -1e30
SCALE = HEAD ** -0.5
LOG2E = 1.4426950408889634
F32 = jnp.float32
BF16 = jnp.bfloat16
VMEM_LIMIT = 48 * 1024 * 1024


def seq_perm(move):
    pairs = []
    for s in range(16):
        z, x, c = s // 8, (s // 2) % 4, s % 2
        nz, nx, nc = move(z, x, c)
        pairs.append((s, nz * 8 + nx * 2 + nc))
    return pairs


def core_swap(value):
    return lax.ppermute(value, "seq", seq_perm(lambda z, x, c: (z, x, 1 - c)))


def x_shift(value, by):
    return lax.ppermute(value, "seq", seq_perm(lambda z, x, c: (z, (x + by) % 4, c)))


def z_swap(value):
    return lax.ppermute(value, "seq", seq_perm(lambda z, x, c: (1 - z, x, c)))


def nt(a, b):
    return lax.dot_general(a, b, (((1,), (1,)), ((), ())), preferred_element_type=F32)


def nn(a, b):
    return lax.dot_general(a, b, (((1,), (0,)), ((), ())), preferred_element_type=F32)


def tn(a, b):
    return lax.dot_general(a, b, (((0,), (0,)), ((), ())), preferred_element_type=F32)


def fill(own_ref, pieces, kv_scr, bias_scr):
    own = own_ref[0]
    z, x, c = own // 8, (own // 2) % 4, own % 2
    key_at = lax.broadcasted_iota(jnp.int32, (ROWS, ROWS), 0)
    query_at = lax.broadcasted_iota(jnp.int32, (ROWS, ROWS), 1)
    lag = key_at - query_at
    query_doc = pieces[0][0, ROWS:ROWS + 1, :ROWS].astype(F32)
    for n, piece in enumerate(pieces):
        other, k = n // 4, n % 4
        for part in range(2):
            at = (2 * n + part) * ROWS
            kv_scr[at:at + ROWS, :] = piece[part, :ROWS, :]
            block = ((z + part) % 2) * 8 + ((x + 4 - k) % 4) * 2 + (c + other) % 2
            doc = piece[part, ROWS:ROWS + 8, :ROWS].astype(F32)
            doc = jnp.broadcast_to(doc[:1, :], (ROWS, ROWS)).T
            allowed = (doc == query_doc) & (lag <= (own - block) * ROWS)
            bias_scr[at:at + ROWS, :] = jnp.where(allowed, 0.0, NEG)


def stack_heads(ref, kv):
    return jnp.concatenate(
        [ref[:, (kv * 4 + g) * HEAD:(kv * 4 + g + 1) * HEAD] for g in range(4)], axis=0
    )


def forward_kernel(own_ref, q_ref, *refs):
    pieces, (o_ref, lse_ref, kv_scr, bias_scr, s_scr) = refs[:8], refs[8:]
    fill(own_ref, pieces, kv_scr, bias_scr)
    step = 256
    count = kv_scr.shape[0] // step
    for kv in range(2):
        q = stack_heads(q_ref, kv)

        def scores(i, top):
            rows = pl.ds(pl.multiple_of(i * step, step), step)
            bias = bias_scr[rows, :]
            s = nt(kv_scr[rows, kv * HEAD:(kv + 1) * HEAD], q)
            s = s + jnp.concatenate([bias] * 4, axis=1)
            s_scr[rows, :] = s
            return jnp.maximum(top, jnp.max(s.reshape(step // 8, 8, 512), axis=0))

        top = lax.fori_loop(0, count, scores, jnp.full((8, 512), NEG, F32))
        top = jnp.max(top, axis=0, keepdims=True)

        def values(i, state):
            total, acc = state
            rows = pl.ds(pl.multiple_of(i * step, step), step)
            p = jnp.exp2((s_scr[rows, :] - top) * (SCALE * LOG2E))
            v = kv_scr[rows, 256 + kv * HEAD:256 + (kv + 1) * HEAD]
            total = total + jnp.sum(p.reshape(step // 8, 8, 512), axis=0)
            return total, acc + tn(v, p.astype(BF16))

        total, acc = lax.fori_loop(
            0, count, values, (jnp.zeros((8, 512), F32), jnp.zeros((HEAD, 512), F32))
        )
        total = jnp.sum(total, axis=0, keepdims=True)
        out = (acc / total).T.astype(BF16)
        for g in range(4):
            o_ref[:, (kv * 4 + g) * HEAD:(kv * 4 + g + 1) * HEAD] = out[g * ROWS:(g + 1) * ROWS]
        lse = top * (SCALE * LOG2E) + jnp.log2(total)
        lse_ref[kv * 8:(kv + 1) * 8, :] = jnp.broadcast_to(lse, (8, 512))


def backward_kernel(own_ref, q_ref, d_ref, o_ref, lse_ref, *refs):
    pieces, (dq_ref, own_out, sib_out, kv_scr, bias_scr) = refs[:8], refs[8:]
    fill(own_ref, pieces, kv_scr, bias_scr)
    step = 256
    for kv in range(2):
        q = stack_heads(q_ref, kv)
        d = stack_heads(d_ref, kv)
        o = stack_heads(o_ref, kv)
        lse = lse_ref[kv * 8:kv * 8 + 1, :]
        product = d.astype(F32) * o.astype(F32)
        delta = jnp.sum(product.T, axis=0, keepdims=True)

        def half(out_ref, base):
            def tile(i, acc):
                rows = pl.ds(pl.multiple_of(base + i * step, step), step)
                k = kv_scr[rows, kv * HEAD:(kv + 1) * HEAD]
                v = kv_scr[rows, 256 + kv * HEAD:256 + (kv + 1) * HEAD]
                bias = bias_scr[rows, :]
                s = nt(k, q) * (SCALE * LOG2E) - lse
                p = jnp.exp2(s + jnp.concatenate([bias] * 4, axis=1))
                dp = nt(v, d)
                ds = (p * (dp - delta) * SCALE).astype(BF16)
                out_ref[i, :, kv * HEAD:(kv + 1) * HEAD] = nn(ds, q).astype(BF16)
                out_ref[i, :, 256 + kv * HEAD:256 + (kv + 1) * HEAD] = nn(
                    p.astype(BF16), d
                ).astype(BF16)
                return acc + tn(k, ds)

            return tile

        acc = lax.fori_loop(0, 4, half(own_out, 0), jnp.zeros((HEAD, 512), F32))
        acc = lax.fori_loop(0, 4, half(sib_out, 1024), acc)
        dq = acc.T
        for g in range(4):
            dq_ref[:, (kv * 4 + g) * HEAD:(kv * 4 + g + 1) * HEAD] = dq[g * ROWS:(g + 1) * ROWS]


def weight_kernel(z_ref, *refs):
    heads, grads, (out_ref, h_scr, g_scr) = refs[:8], refs[8:12], refs[12:]
    z = z_ref[0]
    for n in range(8):
        other, k = n // 4, n % 4
        h_scr[n * ROWS:(n + 1) * ROWS, :] = heads[n][...]
        for part in range(2):
            g_scr[part, n * ROWS:(n + 1) * ROWS, :] = grads[k][other, part]

    def piece(k, carry):
        to = (z + k) % 8
        lanes = pl.ds(pl.multiple_of((to % 4) * 256, 256), 256)
        out_ref[k] = tn(h_scr[:, lanes], g_scr[to // 4]).astype(BF16)
        return carry

    lax.fori_loop(0, 8, piece, 0)


SMEM = pl.BlockSpec(memory_space=pltpu.SMEM)
VMEM = pl.BlockSpec(memory_space=pltpu.VMEM)


def call(kernel, inputs, out_shape, scratch, flops, size):
    return pl.pallas_call(
        kernel,
        out_shape=out_shape,
        in_specs=[SMEM] + [VMEM] * (len(inputs) - 1),
        out_specs=jax.tree.map(lambda _: VMEM, out_shape),
        scratch_shapes=scratch,
        compiler_params=pltpu.CompilerParams(vmem_limit_bytes=VMEM_LIMIT),
        cost_estimate=pl.CostEstimate(flops=flops, bytes_accessed=size, transcendentals=0),
    )(*inputs)


def shards(queries, keys, values, grad_out, doc_ids, out_weight):
    rows = queries.shape[1]
    depth = out_weight.shape[0]
    index = lax.axis_index("seq")
    layer = lax.axis_index("dp")
    z, x, c = index // 8, (index // 2) % 4, index % 2
    own = index.astype(jnp.int32).reshape(1)
    height = (z * 4 + layer).astype(jnp.int32).reshape(1)
    shape = jax.ShapeDtypeStruct

    docs = jnp.tile(doc_ids[0].astype(BF16)[None, :], (16, 4))
    message = jnp.concatenate([jnp.concatenate([keys[0], values[0]], axis=1), docs], axis=0)
    base = jnp.stack([message, z_swap(message)])
    mine = [base] + [x_shift(base, k) for k in (1, 2, 3)]
    pieces = mine + [core_swap(piece) for piece in mine]

    full = lax.all_gather(grad_out[0], "head", axis=0)
    head_grad = sum(
        lax.dot_general(
            full[y], out_weight[:, y * 1024:(y + 1) * 1024], (((1,), (1,)), ((), ())),
            preferred_element_type=F32,
        )
        for y in range(4)
    ).astype(BF16)
    split = full.reshape(2, 2, rows, 2, 2, 256)
    keep = lax.dynamic_index_in_dim(split, c, axis=4, keepdims=False)
    give = lax.dynamic_index_in_dim(split, 1 - c, axis=4, keepdims=False)
    both = jnp.stack([keep, core_swap(give)])
    grads = []
    for k in range(4):
        to = (x + k) % 4
        part = lax.dynamic_index_in_dim(both, to // 2, axis=2, keepdims=False)
        part = lax.dynamic_index_in_dim(part, to % 2, axis=3, keepdims=False)
        grads.append(part if k == 0 else x_shift(part, k))

    q = queries[0]
    tokens = 2048
    heads, lse = call(
        forward_kernel,
        [own, q] + pieces,
        (shape((rows, depth), BF16), shape((16, 512), F32)),
        [
            pltpu.VMEM((tokens, 512), BF16),
            pltpu.VMEM((tokens, ROWS), F32),
            pltpu.VMEM((tokens, 512), F32),
        ],
        2 * 2 * 1024 * 2048 * 128,
        4 << 20,
    )

    near = [heads] + [x_shift(heads, k) for k in (1, 2, 3)]
    far = [core_swap(piece) for piece in near]
    products = call(
        weight_kernel,
        [height] + near + far + grads,
        shape((8, 256, 256), BF16),
        [pltpu.VMEM((1024, depth), BF16), pltpu.VMEM((2, 1024, 256), BF16)],
        2 * 1024 * 1024 * 512,
        4 << 20,
    )
    total = products[0].astype(F32)
    for k in range(1, 8):
        pairs = []
        for at in range(8):
            to = (at + k) % 8
            for r in range(8):
                pairs.append(((at % 4) * 16 + (at // 4) * 8 + r, (to % 4) * 16 + (to // 4) * 8 + r))
        total = total + lax.ppermute(products[k], ("dp", "seq"), pairs).astype(F32)
    mine_w = total.astype(BF16)
    weight_grad = jnp.zeros((4, 256, 256), BF16)
    weight_grad = lax.dynamic_update_index_in_dim(weight_grad, mine_w, layer, 0)
    for k in range(1, 4):
        came = lax.ppermute(mine_w, "dp", [(i, (i + k) % 4) for i in range(4)])
        weight_grad = lax.dynamic_update_index_in_dim(weight_grad, came, (layer + 4 - k) % 4, 0)
    weight_grad = weight_grad.reshape(1024, 256).astype(F32)

    terms = jnp.dot(heads, out_weight, preferred_element_type=F32).astype(BF16)
    layer_out = lax.psum_scatter(terms, "head", scatter_dimension=1, tiled=True).astype(F32)

    grad_query, kept, given = call(
        backward_kernel,
        [own, q, head_grad, heads, lse] + pieces,
        (shape((rows, depth), F32), shape((4, 256, 512), BF16), shape((4, 256, 512), BF16)),
        [pltpu.VMEM((tokens, 512), BF16), pltpu.VMEM((tokens, ROWS), F32)],
        5 * 2 * 1024 * 2048 * 128,
        8 << 20,
    )
    summed = (kept.astype(F32) + core_swap(given).astype(F32)).astype(BF16)
    along = summed[0].astype(F32)
    for k in (1, 2, 3):
        along = along + x_shift(summed[k], -k).astype(F32)
    final = along[:ROWS] + z_swap(along[ROWS:].astype(BF16)).astype(F32)
    return (
        layer_out[None],
        grad_query[None],
        final[:, :256][None],
        final[:, 256:][None],
        weight_grad,
    )


def solution(mesh):
    placed = (
        P("dp", "seq", "head"),
        P("dp", "seq", "head"),
        P("dp", "seq", "head"),
        P("dp", "seq", "head"),
        P("dp", "seq"),
        P("head", None),
    )
    return jax.shard_map(
        shards,
        mesh=mesh,
        in_specs=placed,
        out_specs=(
            P("dp", "seq", "head"),
            P("dp", "seq", "head"),
            P("dp", "seq", "head"),
            P("dp", "seq", "head"),
            P("head", "seq"),
        ),
        check_vma=False,
    )
```

time: 784 us -> 184 us (0.23)
  waiting for transfers between devices: 598 us -> 56.9 us
  blocking collectives: 56.3 us -> 0 us
  starting transfers between devices: 4.64 us -> 53.5 us
  matrix products: 35.2 us -> 11.6 us
  Pallas kernels: 0 us -> 23.5 us
  local copies, waits for them, and re-layouts: 33.6 us -> 14.2 us
  other arithmetic: 25.6 us -> 7.34 us
  loops' own time: 12.7 us -> 0 us
    ppermute x96 -> x34, waiting for transfers between devices: 314 us -> 56.2 us  [the longest x12 25.9 us: x_shift(): lax.ppermute(value, 'seq', seq_perm(lambda z, x, c: (z, (x + by) % 4, c)))]
    reduce_scatter x2 -> x1, waiting for transfers between devices: 210 us -> 0.01 us  [shards(): lax.psum_scatter(terms, 'head', scatter_dimension=1, tiled=True).astype(F32)]
    all_gather x3 -> x1, waiting for transfers between devices: 73.2 us -> 0.01 us  [shards(): full = lax.all_gather(grad_out[0], 'head', axis=0)]
    all_gather x2 -> x0, blocking collectives: 56.3 us -> none  [the longest x1 32.1 us: shards(): lax.all_gather(positions, 'seq', axis=0, tiled=True)]
    ppermute x96 -> x34, starting transfers between devices: 4.4 us -> 53.4 us  [the longest x12 19.7 us: x_shift(): lax.ppermute(value, 'seq', seq_perm(lambda z, x, c: (z, (x + by) % 4, c)))]
    dot_general x10 -> x5, matrix products: 35.2 us -> 11.6 us  [the longest x4 5.97 us: shards(): lax.dot_general(full[y], out_weight[:, y * 1024:(y + 1) * 1024], (((1,),...]
    pallas_call x0 -> x3, Pallas kernels: none -> 23.5 us  [call(): pl.pallas_call(kernel, out_shape=out_shape, in_specs=[SMEM] + [VMEM] * (l...]
    while x67 -> x0, local copies, waits for them, and re-layouts: 20.8 us -> none
  transfers between devices with their start and end apart: 102 -> 36, of which waited for: 51 -> 17; matrix products, arithmetic and copies ran while one was open for 8% -> 14% of each run, Pallas kernels for 0% -> 13%
where the time goes in v1:
time: 184 us; the launch traced here: 182 us
  waiting for transfers between devices  56.9 us (31%)
  starting transfers between devices  53.5 us (29%)
  Pallas kernels  23.5 us (13%)
  between operations  14.5 us (8%)
  local copies, waits for them, and re-layouts  14.2 us (8%)
  matrix products  11.6 us (6%)
  other arithmetic  7.34 us (4%)
    ppermute x12, waiting for transfers between devices, x_shift(): lax.ppermute(value, 'seq', seq_perm(lambda z, x, c: (z, (x + by) % 4, c)))  25.9 us
    pallas_call x3, Pallas kernels, call(): pl.pallas_call(kernel, out_shape=out_shape, in_specs=[SMEM] + [VMEM] * (l...  23.5 us
    ppermute x12, starting transfers between devices, x_shift(): lax.ppermute(value, 'seq', seq_perm(lambda z, x, c: (z, (x + by) % 4, c)))  19.7 us
    ppermute x7, starting transfers between devices, shards(): total = total + lax.ppermute(products[k], ('dp', 'seq'), pairs).astype(F32)  19.4 us
    ppermute x2, waiting for transfers between devices, z_swap(): return lax.ppermute(value, 'seq', seq_perm(lambda z, x, c: (1 - z, x, c)))  12.8 us
    ppermute x7, waiting for transfers between devices, shards(): total = total + lax.ppermute(products[k], ('dp', 'seq'), pairs).astype(F32)  10 us
    ppermute x2, starting transfers between devices, z_swap(): return lax.ppermute(value, 'seq', seq_perm(lambda z, x, c: (1 - z, x, c)))  9.95 us
    unnamed x44, local copies, waits for them, and re-layouts  6.6 us
  transfers between devices with their start and end apart: 36, of which 17 were waited for; matrix products, arithmetic and copies ran while one was open for 14% of the time, Pallas kernels for 13%

profile of v1, /device:TPU:56, one launch (start us, length us, event | category | flops | bytes accessed | tf_op | source)
XLA Modules:
  0.0 181.6 jit_solution(4578101226521276107)
XLA Ops:
  9.5 6.4 %collective-permute-start = (bf16[144,512]{1,0:T(8,128)(2,1)S(1)}, bf16[144,512]{1,0:T(8,128)(2,1)S(1)}, u32[]{:S(2)}, u32[]{:S(2)}) collective-permute-start(bf16[144,512]{1,0:T(8,128)(2,1)S(1)} %get-tuple-element.36), channel_id=1, source_target_pairs={{0,32},{4,36},{8,40},{12,44},{16,48},{20,52},{24,56},{28,60},{32,0... | collective-permute-start | bytes 442376 | tf_op jit(solution)/shard_map/ppermute | solution.py:38
  15.9 7.1 %collective-permute-done = bf16[144,512]{1,0:T(8,128)(2,1)S(1)} collective-permute-done((bf16[144,512]{1,0:T(8,128)(2,1)S(1)}, bf16[144,512]{1,0:T(8,128)(2,1)S(1)}, u32[]{:S(2)}, u32[]{:S(2)}) %collective-permute-start) | collective-permute-done | bytes 147488 | tf_op jit(solution)/shard_map/ppermute | solution.py:38
  24.5 2.7 %collective-permute-start.2 = (bf16[2,144,512]{2,1,0:T(8,128)(2,1)S(1)}, bf16[2,144,512]{2,1,0:T(8,128)(2,1)S(1)}, u32[]{:S(2)}, u32[]{:S(2)}) collective-permute-start(bf16[2,144,512]{2,1,0:T(8,128)(2,1)S(1)} %pad_maximum_fusion.refs_0_), channel_id=1, source_target_pairs={{0,16},{4,20},{8,24},{12,28},{16,0},{20,4},{24,8},{28,12},{32,48},... | collective-permute-start | bytes 884744 | tf_op jit(solution)/shard_map/ppermute | solution.py:34
  28.7 4.5 %collective-permute-done.1.refs_1_ = bf16[2,144,512]{2,1,0:T(8,128)(2,1)S(1)} collective-permute-done((bf16[2,144,512]{2,1,0:T(8,128)(2,1)S(1)}, bf16[2,144,512]{2,1,0:T(8,128)(2,1)S(1)}, u32[]{:S(2)}, u32[]{:S(2)}) %collective-permute-start.1) | collective-permute-done | bytes 294944 | tf_op jit(solution)/shard_map/ppermute | solution.py:34
  33.2 6.4 %collective-permute-done.2.refs_2_ = bf16[2,144,512]{2,1,0:T(8,128)(2,1)S(1)} collective-permute-done((bf16[2,144,512]{2,1,0:T(8,128)(2,1)S(1)}, bf16[2,144,512]{2,1,0:T(8,128)(2,1)S(1)}, u32[]{:S(2)}, u32[]{:S(2)}) %collective-permute-start.2) | collective-permute-done | bytes 294944 | tf_op jit(solution)/shard_map/ppermute | solution.py:34
  42.7 8.4 %shard_map.101 = (bf16[128,1024]{1,0:T(8,128)(2,1)S(1)}, f32[16,512]{1,0:T(8,128)S(1)}) custom-call(s32[1]{0:T(128)} %bitcast.own_ref, bf16[128,1024]{1,0:T(8,128)(2,1)S(1)} %bitcast.91, bf16[2,144,512]{2,1,0:T(8,128)(2,1)S(1)} %pad_maximum_fusion.refs_0_, bf16[2,144,512]{2,1,0:T(8,128)(2,1)S(1)} %collective-permute-done.1.refs_1_, ...), custom_call_target="tpu_custom_call" | custom-call | flops 1073741824 | bytes 4194304 | tf_op jit(solution)/shard_map/pallas_call | solution.py:176
  56.2 5.4 %collective-permute-done.13.refs_1_ = bf16[128,1024]{1,0:T(8,128)(2,1)S(1)} collective-permute-done((bf16[128,1024]{1,0:T(8,128)(2,1)S(1)}, bf16[128,1024]{1,0:T(8,128)(2,1)S(1)}, u32[]{:S(2)}, u32[]{:S(2)}) %collective-permute-start.13) | collective-permute-done | bytes 262176 | tf_op jit(solution)/shard_map/ppermute | solution.py:34
  61.6 5.0 %collective-permute-done.14.refs_2_ = bf16[128,1024]{1,0:T(8,128)(2,1)S(1)} collective-permute-done((bf16[128,1024]{1,0:T(8,128)(2,1)S(1)}, bf16[128,1024]{1,0:T(8,128)(2,1)S(1)}, u32[]{:S(2)}, u32[]{:S(2)}) %collective-permute-start.14) | collective-permute-done | bytes 262176 | tf_op jit(solution)/shard_map/ppermute | solution.py:34
  67.1 2.6 %reshape.46 = bf16[2,2,128,2,2,256]{5,4,3,2,1,0:T(2,128)(2,1)} reshape(bf16[4,128,1024]{2,1,0:T(8,128)(2,1)} %all-gather.2.cloned.1.call-done) | data formatting | bytes 2097152 | tf_op jit(solution)/shard_map/reshape | solution.py:211
  69.8 3.9 %constant_dynamic-slice_fusion = (bf16[2,2,128,2,1,256]{5,4,3,2,1,0:T(2,128)(2,1)S(1)}, bf16[2,2,128,2,1,256]{5,4,3,2,1,0:T(2,128)(2,1)S(1)}) fusion(bf16[2,2,128,2,2,256]{5,4,3,2,1,0:T(2,128)(2,1)} %reshape.46, s32[]{:T(128)S(6)} %select_n.139, s32[]{:T(128)S(6)} %select_n.138), kind=kLoop, calls=%fused_computation.71 | loop fusion | bytes 2097160 | tf_op jit(solution)/shard_map/jit(dynamic_index_in_dim)/dynamic_slice | solution.py:213
  81.4 2.5 %collective-permute-start.22 = (bf16[2,2,128,256]{3,2,1,0:T(8,128)(2,1)S(1)}, bf16[2,2,128,256]{3,2,1,0:T(8,128)(2,1)S(1)}, u32[]{:S(2)}, u32[]{:S(2)}) collective-permute-start(bf16[2,2,128,256]{3,2,1,0:T(8,128)(2,1)S(1)} %get-tuple-element.27), channel_id=1, source_target_pairs={{0,16},{4,20},{8,24},{12,28},{16,0},{20,4},{24,8},{28,12},{32,48},... | collective-permute-start | bytes 786440 | tf_op jit(solution)/shard_map/ppermute | solution.py:34
  88.5 10.9 %shard_map.102 = (f32[128,1024]{1,0:T(8,128)}, bf16[4,256,512]{2,1,0:T(8,128)(2,1)S(1)}, bf16[4,256,512]{2,1,0:T(8,128)(2,1)}) custom-call(s32[1]{0:T(128)} %bitcast.own_ref, bf16[128,1024]{1,0:T(8,128)(2,1)S(1)} %bitcast.92, bf16[128,1024]{1,0:T(8,128)(2,1)S(1)} %fusion.17.d_ref, bf16[128,1024]{1,0:T(8,128)(2,1)S(1)} %get-tuple-element.10.o_ref.refs_0_, ...), custom_call_target="tpu_custom_call" | custom-call | flops 2684354560 | bytes 8388608 | tf_op jit(solution)/shard_map/pallas_call | solution.py:176
  102.0 4.2 %shard_map.103 = bf16[8,256,256]{2,1,0:T(8,128)(2,1)S(1)} custom-call(s32[1]{0:T(128)} %bitcast.20.z_ref, bf16[128,1024]{1,0:T(8,128)(2,1)S(1)} %get-tuple-element.10.o_ref.refs_0_, bf16[128,1024]{1,0:T(8,128)(2,1)S(1)} %collective-permute-done.13.refs_1_, bf16[128,1024]{1,0:T(8,128)(2,1)S(1)} %collective-permute-done.14.refs_2_, ...), custom_call_target="tpu_custom_call" | custom-call | flops 1073741824 | bytes 4194304 | tf_op jit(solution)/shard_map/pallas_call | solution.py:176
  106.6 5.6 %collective-permute-start.29 = (bf16[256,256]{1,0:T(8,128)(2,1)S(1)}, bf16[256,256]{1,0:T(8,128)(2,1)S(1)}, u32[]{:S(2)}, u32[]{:S(2)}) collective-permute-start(bf16[256,256]{1,0:T(8,128)(2,1)S(1)} %get-tuple-element.19), channel_id=1, source_target_pairs={{0,160},{4,164},{8,168},{12,172},{16,176},{20,180},{24,184},{28,18... | collective-permute-start | bytes 393224 | tf_op jit(solution)/shard_map/ppermute | solution.py:254
  112.6 3.9 %collective-permute-start.27 = (bf16[256,256]{1,0:T(8,128)(2,1)S(1)}, bf16[256,256]{1,0:T(8,128)(2,1)S(1)}, u32[]{:S(2)}, u32[]{:S(2)}) collective-permute-start(bf16[256,256]{1,0:T(8,128)(2,1)S(1)} %get-tuple-element.21), channel_id=1, source_target_pairs={{0,32},{4,36},{8,40},{12,44},{16,48},{20,52},{24,56},{28,60},{64,9... | collective-permute-start | bytes 393224 | tf_op jit(solution)/shard_map/ppermute | solution.py:254
  118.1 3.7 %collective-permute-done.29 = bf16[256,256]{1,0:T(8,128)(2,1)S(1)} collective-permute-done((bf16[256,256]{1,0:T(8,128)(2,1)S(1)}, bf16[256,256]{1,0:T(8,128)(2,1)S(1)}, u32[]{:S(2)}, u32[]{:S(2)}) %collective-permute-start.29) | collective-permute-done | bytes 131104 | tf_op jit(solution)/shard_map/ppermute | solution.py:254
  123.5 7.1 %collective-permute-start.24 = (bf16[256,256]{1,0:T(8,128)(2,1)S(1)}, bf16[256,256]{1,0:T(8,128)(2,1)}, u32[]{:S(2)}, u32[]{:S(2)}) collective-permute-start(bf16[256,256]{1,0:T(8,128)(2,1)S(1)} %get-tuple-element.17), channel_id=1, source_target_pairs={{0,64},{4,68},{8,72},{12,76},{16,80},{20,84},{24,88},{28,92},{64,1... | collective-permute-start | bytes 393224 | tf_op jit(solution)/shard_map/ppermute | solution.py:254
  130.6 5.6 %convolution_convert_fusion = bf16[128,4096]{1,0:T(8,128)(2,1)} fusion(bf16[128,1024]{1,0:T(8,128)(2,1)S(1)} %get-tuple-element.10.o_ref.refs_0_, bf16[1024,4096]{1,0:T(8,128)(2,1)} %param.11), kind=kOutput, calls=%fused_computation | convolution fusion | flops 1074266112 | bytes 9699328 | tf_op jit(solution)/shard_map/dot_general | solution.py:263
  138.7 2.8 %collective-permute-done.24 = bf16[256,256]{1,0:T(8,128)(2,1)} collective-permute-done((bf16[256,256]{1,0:T(8,128)(2,1)S(1)}, bf16[256,256]{1,0:T(8,128)(2,1)}, u32[]{:S(2)}, u32[]{:S(2)}) %collective-permute-start.24) | collective-permute-done | bytes 131104 | tf_op jit(solution)/shard_map/ppermute | solution.py:254
  151.6 3.3 %collective-permute-done.32 = bf16[256,256]{1,0:T(8,128)(2,1)S(1)} collective-permute-done((bf16[256,256]{1,0:T(8,128)(2,1)S(1)}, bf16[256,256]{1,0:T(8,128)(2,1)S(1)}, u32[]{:S(2)}, u32[]{:S(2)}) %collective-permute-start.32) | collective-permute-done | bytes 131104 | tf_op jit(solution)/shard_map/ppermute | solution.py:259
  154.9 2.7 %collective-permute-done.33 = bf16[256,256]{1,0:T(8,128)(2,1)S(1)} collective-permute-done((bf16[256,256]{1,0:T(8,128)(2,1)S(1)}, bf16[256,256]{1,0:T(8,128)(2,1)S(1)}, u32[]{:S(2)}, u32[]{:S(2)}) %collective-permute-start.33) | collective-permute-done | bytes 131104 | tf_op jit(solution)/shard_map/ppermute | solution.py:259
  158.7 3.3 %collective-permute-done.11 = bf16[256,512]{1,0:T(8,128)(2,1)S(1)} collective-permute-done((bf16[256,512]{1,0:T(8,128)(2,1)S(1)}, bf16[256,512]{1,0:T(8,128)(2,1)S(1)}, u32[]{:S(2)}, u32[]{:S(2)}) %collective-permute-start.11) | collective-permute-done | bytes 262176 | tf_op jit(solution)/shard_map/ppermute | solution.py:34
  162.8 3.6 %collective-permute-start.12 = (bf16[128,512]{1,0:T(8,128)(2,1)S(1)}, bf16[128,512]{1,0:T(8,128)(2,1)S(1)}, u32[]{:S(2)}, u32[]{:S(2)}) collective-permute-start(bf16[128,512]{1,0:T(8,128)(2,1)S(1)} %slice.161), channel_id=1, source_target_pairs={{0,32},{4,36},{8,40},{12,44},{16,48},{20,52},{24,56},{28,60},{32,0... | collective-permute-start | bytes 393224 | tf_op jit(solution)/shard_map/ppermute | solution.py:38
  168.2 5.8 %collective-permute-done.12 = bf16[128,512]{1,0:T(8,128)(2,1)S(1)} collective-permute-done((bf16[128,512]{1,0:T(8,128)(2,1)S(1)}, bf16[128,512]{1,0:T(8,128)(2,1)S(1)}, u32[]{:S(2)}, u32[]{:S(2)}) %collective-permute-start.12) | collective-permute-done | bytes 131104 | tf_op jit(solution)/shard_map/ppermute | solution.py:38
  (126 shorter events, 49.6 us)
Async XLA Ops:
  7.2 60.0 %all-gather.2.cloned.1.call-start = ((), (), s32[]{:S(2)}) async-start(), calls=%async_computation.2 | async-start | bytes 1310720 | tf_op jit(solution)/shard_map/all_gather | solution.py:203
  7.9 158.5 %reduce-scatter.2.cloned.1.call-start = ((), (), s32[]{:S(2)}) async-start(), calls=%async_computation.1 | async-start | bytes 1310720 | tf_op jit(solution)/shard_map/reduce_scatter | solution.py:264
  9.5 13.4 %collective-permute-start = (bf16[144,512]{1,0:T(8,128)(2,1)S(1)}, bf16[144,512]{1,0:T(8,128)(2,1)S(1)}, u32[]{:S(2)}, u32[]{:S(2)}) collective-permute-start(bf16[144,512]{1,0:T(8,128)(2,1)S(1)} %get-tuple-element.36), channel_id=1, source_target_pairs={{0,32},{4,36},{8,40},{12,44},{16,48},{20,52},{24,56},{28,60},{32,0... | collective-permute-start | bytes 442376 | tf_op jit(solution)/shard_map/ppermute | solution.py:38
  24.5 15.1 %collective-permute-start.2 = (bf16[2,144,512]{2,1,0:T(8,128)(2,1)S(1)}, bf16[2,144,512]{2,1,0:T(8,128)(2,1)S(1)}, u32[]{:S(2)}, u32[]{:S(2)}) collective-permute-start(bf16[2,144,512]{2,1,0:T(8,128)(2,1)S(1)} %pad_maximum_fusion.refs_0_), channel_id=1, source_target_pairs={{0,16},{4,20},{8,24},{12,28},{16,0},{20,4},{24,8},{28,12},{32,48},... | collective-permute-start | bytes 884744 | tf_op jit(solution)/shard_map/ppermute | solution.py:34
  27.3 12.4 %collective-permute-start.3 = (bf16[2,144,512]{2,1,0:T(8,128)(2,1)S(1)}, bf16[2,144,512]{2,1,0:T(8,128)(2,1)S(1)}, u32[]{:S(2)}, u32[]{:S(2)}) collective-permute-start(bf16[2,144,512]{2,1,0:T(8,128)(2,1)S(1)} %pad_maximum_fusion.refs_0_), channel_id=1, source_target_pairs={{0,24},{4,28},{8,0},{12,4},{16,8},{20,12},{24,16},{28,20},{32,56},... | collective-permute-start | bytes 884744 | tf_op jit(solution)/shard_map/ppermute | solution.py:34
  52.2 14.4 %collective-permute-start.14 = (bf16[128,1024]{1,0:T(8,128)(2,1)S(1)}, bf16[128,1024]{1,0:T(8,128)(2,1)S(1)}, u32[]{:S(2)}, u32[]{:S(2)}) collective-permute-start(bf16[128,1024]{1,0:T(8,128)(2,1)S(1)} %get-tuple-element.10.o_ref.refs_0_), channel_id=1, source_target_pairs={{0,16},{4,20},{8,24},{12,28},{16,0},{20,4},{24,8},{28,12},{32,48},... | collective-permute-start | bytes 786440 | tf_op jit(solution)/shard_map/ppermute | solution.py:34
  54.6 12.5 %collective-permute-start.15 = (bf16[128,1024]{1,0:T(8,128)(2,1)S(1)}, bf16[128,1024]{1,0:T(8,128)(2,1)S(1)}, u32[]{:S(2)}, u32[]{:S(2)}) collective-permute-start(bf16[128,1024]{1,0:T(8,128)(2,1)S(1)} %get-tuple-element.10.o_ref.refs_0_), channel_id=1, source_target_pairs={{0,24},{4,28},{8,0},{12,4},{16,8},{20,12},{24,16},{28,20},{32,56},... | collective-permute-start | bytes 786440 | tf_op jit(solution)/shard_map/ppermute | solution.py:34
  56.2 25.2 %collective-permute-start.16 = (bf16[128,1024]{1,0:T(8,128)(2,1)S(1)}, bf16[128,1024]{1,0:T(8,128)(2,1)S(1)}, u32[]{:S(2)}, u32[]{:S(2)}) collective-permute-start(bf16[128,1024]{1,0:T(8,128)(2,1)S(1)} %get-tuple-element.10.o_ref.refs_0_), channel_id=1, source_target_pairs={{0,4},{4,0},{8,12},{12,8},{16,20},{20,16},{24,28},{28,24},{32,36},... | collective-permute-start | bytes 786440 | tf_op jit(solution)/shard_map/ppermute | solution.py:30
  61.6 22.4 %collective-permute-start.17 = (bf16[128,1024]{1,0:T(8,128)(2,1)S(1)}, bf16[128,1024]{1,0:T(8,128)(2,1)S(1)}, u32[]{:S(2)}, u32[]{:S(2)}) collective-permute-start(bf16[128,1024]{1,0:T(8,128)(2,1)S(1)} %collective-permute-done.13.refs_1_), channel_id=1, source_target_pairs={{0,4},{4,0},{8,12},{12,8},{16,20},{20,16},{24,28},{28,24},{32,36},... | collective-permute-start | bytes 786440 | tf_op jit(solution)/shard_map/ppermute | solution.py:30
  66.6 32.8 %collective-permute-start.18 = (bf16[128,1024]{1,0:T(8,128)(2,1)S(1)}, bf16[128,1024]{1,0:T(8,128)(2,1)S(1)}, u32[]{:S(2)}, u32[]{:S(2)}) collective-permute-start(bf16[128,1024]{1,0:T(8,128)(2,1)S(1)} %collective-permute-done.14.refs_2_), channel_id=1, source_target_pairs={{0,4},{4,0},{8,12},{12,8},{16,20},{20,16},{24,28},{28,24},{32,36},... | collective-permute-start | bytes 786440 | tf_op jit(solution)/shard_map/ppermute | solution.py:30
  67.1 32.9 %collective-permute-start.19 = (bf16[128,1024]{1,0:T(8,128)(2,1)S(1)}, bf16[128,1024]{1,0:T(8,128)(2,1)}, u32[]{:S(2)}, u32[]{:S(2)}) collective-permute-start(bf16[128,1024]{1,0:T(8,128)(2,1)S(1)} %collective-permute-done.15.refs_3_), channel_id=1, source_target_pairs={{0,4},{4,0},{8,12},{12,8},{16,20},{20,16},{24,28},{28,24},{32,36},... | collective-permute-start | bytes 786440 | tf_op jit(solution)/shard_map/ppermute | solution.py:30
  79.8 20.3 %collective-permute-start.21 = (bf16[2,2,128,256]{3,2,1,0:T(8,128)(2,1)S(1)}, bf16[2,2,128,256]{3,2,1,0:T(8,128)(2,1)S(1)}, u32[]{:S(2)}, u32[]{:S(2)}) collective-permute-start(bf16[2,2,128,256]{3,2,1,0:T(8,128)(2,1)S(1)} %get-tuple-element.26), channel_id=1, source_target_pairs={{0,8},{4,12},{8,16},{12,20},{16,24},{20,28},{24,0},{28,4},{32,40},... | collective-permute-start | bytes 786440 | tf_op jit(solution)/shard_map/ppermute | solution.py:34
  81.4 18.7 %collective-permute-start.22 = (bf16[2,2,128,256]{3,2,1,0:T(8,128)(2,1)S(1)}, bf16[2,2,128,256]{3,2,1,0:T(8,128)(2,1)S(1)}, u32[]{:S(2)}, u32[]{:S(2)}) collective-permute-start(bf16[2,2,128,256]{3,2,1,0:T(8,128)(2,1)S(1)} %get-tuple-element.27), channel_id=1, source_target_pairs={{0,16},{4,20},{8,24},{12,28},{16,0},{20,4},{24,8},{28,12},{32,48},... | collective-permute-start | bytes 786440 | tf_op jit(solution)/shard_map/ppermute | solution.py:34
  84.0 16.1 %collective-permute-start.23 = (bf16[2,2,128,256]{3,2,1,0:T(8,128)(2,1)S(1)}, bf16[2,2,128,256]{3,2,1,0:T(8,128)(2,1)S(1)}, u32[]{:S(2)}, u32[]{:S(2)}) collective-permute-start(bf16[2,2,128,256]{3,2,1,0:T(8,128)(2,1)S(1)} %get-tuple-element.24), channel_id=1, source_target_pairs={{0,24},{4,28},{8,0},{12,4},{16,8},{20,12},{24,16},{28,20},{32,56},... | collective-permute-start | bytes 786440 | tf_op jit(solution)/shard_map/ppermute | solution.py:34
  100.0 45.8 %collective-permute-start.8 = (bf16[4,256,512]{2,1,0:T(8,128)(2,1)}, bf16[4,256,512]{2,1,0:T(8,128)(2,1)}, u32[]{:S(2)}, u32[]{:S(2)}) collective-permute-start(bf16[4,256,512]{2,1,0:T(8,128)(2,1)} %get-tuple-element.14), channel_id=1, source_target_pairs={{0,4},{4,0},{8,12},{12,8},{16,20},{20,16},{24,28},{28,24},{32,36},... | collective-permute-start | bytes 3145736 | tf_op jit(solution)/shard_map/ppermute | solution.py:30
  106.6 15.2 %collective-permute-start.29 = (bf16[256,256]{1,0:T(8,128)(2,1)S(1)}, bf16[256,256]{1,0:T(8,128)(2,1)S(1)}, u32[]{:S(2)}, u32[]{:S(2)}) collective-permute-start(bf16[256,256]{1,0:T(8,128)(2,1)S(1)} %get-tuple-element.19), channel_id=1, source_target_pairs={{0,160},{4,164},{8,168},{12,172},{16,176},{20,180},{24,184},{28,18... | collective-permute-start | bytes 393224 | tf_op jit(solution)/shard_map/ppermute | solution.py:254
  112.6 23.8 %collective-permute-start.27 = (bf16[256,256]{1,0:T(8,128)(2,1)S(1)}, bf16[256,256]{1,0:T(8,128)(2,1)S(1)}, u32[]{:S(2)}, u32[]{:S(2)}) collective-permute-start(bf16[256,256]{1,0:T(8,128)(2,1)S(1)} %get-tuple-element.21), channel_id=1, source_target_pairs={{0,32},{4,36},{8,40},{12,44},{16,48},{20,52},{24,56},{28,60},{64,9... | collective-permute-start | bytes 393224 | tf_op jit(solution)/shard_map/ppermute | solution.py:254
  116.4 19.9 %collective-permute-start.26 = (bf16[256,256]{1,0:T(8,128)(2,1)S(1)}, bf16[256,256]{1,0:T(8,128)(2,1)S(1)}, u32[]{:S(2)}, u32[]{:S(2)}) collective-permute-start(bf16[256,256]{1,0:T(8,128)(2,1)S(1)} %get-tuple-element.22), channel_id=1, source_target_pairs={{0,192},{4,196},{8,200},{12,204},{16,208},{20,212},{24,216},{28,22... | collective-permute-start | bytes 393224 | tf_op jit(solution)/shard_map/ppermute | solution.py:254
  121.8 16.9 %collective-permute-start.25 = (bf16[256,256]{1,0:T(8,128)(2,1)S(1)}, bf16[256,256]{1,0:T(8,128)(2,1)}, u32[]{:S(2)}, u32[]{:S(2)}) collective-permute-start(bf16[256,256]{1,0:T(8,128)(2,1)S(1)} %get-tuple-element.23), channel_id=1, source_target_pairs={{0,128},{4,132},{8,136},{12,140},{16,144},{20,148},{24,152},{28,15... | collective-permute-start | bytes 393224 | tf_op jit(solution)/shard_map/ppermute | solution.py:254
  123.5 18.0 %collective-permute-start.24 = (bf16[256,256]{1,0:T(8,128)(2,1)S(1)}, bf16[256,256]{1,0:T(8,128)(2,1)}, u32[]{:S(2)}, u32[]{:S(2)}) collective-permute-start(bf16[256,256]{1,0:T(8,128)(2,1)S(1)} %get-tuple-element.17), channel_id=1, source_target_pairs={{0,64},{4,68},{8,72},{12,76},{16,80},{20,84},{24,88},{28,92},{64,1... | collective-permute-start | bytes 393224 | tf_op jit(solution)/shard_map/ppermute | solution.py:254
  145.9 11.7 %collective-permute-start.33 = (bf16[256,256]{1,0:T(8,128)(2,1)S(1)}, bf16[256,256]{1,0:T(8,128)(2,1)S(1)}, u32[]{:S(2)}, u32[]{:S(2)}) collective-permute-start(bf16[256,256]{1,0:T(8,128)(2,1)S(1)} %get-tuple-element.16), channel_id=1, source_target_pairs={{0,192},{64,0},{128,64},{192,128},{1,193},{65,1},{129,65},{193,129... | collective-permute-start | bytes 393224 | tf_op jit(solution)/shard_map/ppermute | solution.py:259
  147.5 14.6 %collective-permute-start.11 = (bf16[256,512]{1,0:T(8,128)(2,1)S(1)}, bf16[256,512]{1,0:T(8,128)(2,1)S(1)}, u32[]{:S(2)}, u32[]{:S(2)}) collective-permute-start(bf16[256,512]{1,0:T(8,128)(2,1)S(1)} %get-tuple-element.31), channel_id=1, source_target_pairs={{0,8},{4,12},{8,16},{12,20},{16,24},{20,28},{24,0},{28,4},{32,40},... | collective-permute-start | bytes 786440 | tf_op jit(solution)/shard_map/ppermute | solution.py:34
  148.8 13.2 %collective-permute-start.10 = (bf16[256,512]{1,0:T(8,128)(2,1)S(1)}, bf16[256,512]{1,0:T(8,128)(2,1)S(1)}, u32[]{:S(2)}, u32[]{:S(2)}) collective-permute-start(bf16[256,512]{1,0:T(8,128)(2,1)S(1)} %get-tuple-element.32), channel_id=1, source_target_pairs={{0,16},{4,20},{8,24},{12,28},{16,0},{20,4},{24,8},{28,12},{32,48},... | collective-permute-start | bytes 786440 | tf_op jit(solution)/shard_map/ppermute | solution.py:34
  149.8 12.8 %collective-permute-start.9 = (bf16[256,512]{1,0:T(8,128)(2,1)S(1)}, bf16[256,512]{1,0:T(8,128)(2,1)S(1)}, u32[]{:S(2)}, u32[]{:S(2)}) collective-permute-start(bf16[256,512]{1,0:T(8,128)(2,1)S(1)} %get-tuple-element.30), channel_id=1, source_target_pairs={{0,24},{4,28},{8,0},{12,4},{16,8},{20,12},{24,16},{28,20},{32,56},... | collective-permute-start | bytes 786440 | tf_op jit(solution)/shard_map/ppermute | solution.py:34
  (34 other events, 377.5 us)
Sparse Core Ops, SparseCore 0:
  9.8 27.5 all-gather.1
  136.4 26.9 reduce-scatter.1
